TPU v7x, 32 devices: a whole 2x2x4 slice. The times are simulated.
32 devices in a mesh: dp: 8 (over z, x), mp: 4 (over y, core).
Axes of the slice: x: 2, y: 2, z: 4, core: 2. Of those that a mesh axis runs over, the one named last changes fastest.
Arguments:
- features: bfloat16 [1024, 1536], P('dp', 'mp'), may hold values from -240 to 240
- proj_weight: bfloat16 [1536, 1152], P('mp'), may hold values from -0.15625 to 0.15625
- texts: bfloat16 [1024, 1152], P(('dp', 'mp')), may hold values from -6 to 6
Outputs:
- grad_features: bfloat16 [1024, 1536], P('dp', 'mp')
- grad_weight: float32 [1536, 1152], P('mp')
All inputs are finite; a program needn't handle non-finite values.
Results may differ from a plain program's by a relative error of at most 0.011.
Values may be sent and summed in bfloat16 or wider, within the bound.
No kernel may reach another device: no remote copies, remote signals or barrier semaphores. Data moves between devices by JAX's collectives and lax.ppermute only.
A program may use at most 64 MiB of HBM per device.

v0:
```python
import functools

import jax
import jax.numpy as jnp
from jax import lax
from jax.experimental import pallas as pl
from jax.experimental.pallas import tpu as pltpu
from jax.sharding import PartitionSpec as P

logit_scale = 100.0
logit_bias = -10.0
epsilon = 1e-06
LANES = 128
GATHER_BYTES = 8 << 20
VMEM_BYTES = 40 << 20


def unit_rows(values):
    return values * lax.rsqrt(jnp.sum(values * values, axis=1, keepdims=True) + epsilon)


def add_texts(unit_img_b, image_ids, piece, piece_ids):
    unit_txt_b = unit_rows(piece.astype(jnp.float32)).astype(jnp.bfloat16)
    logits = (
        logit_scale * jnp.dot(unit_img_b, unit_txt_b.T, preferred_element_type=jnp.float32)
        + logit_bias
    )
    labels = jnp.where(image_ids[:, None] == piece_ids[None, :], 1.0, -1.0).astype(jnp.float32)
    slopes = (-labels * jax.nn.sigmoid(-labels * logits)).astype(jnp.bfloat16)
    return logit_scale * jnp.dot(slopes, unit_txt_b, preferred_element_type=jnp.float32)


def shards_summed(features, proj_weight, texts):
    local_rows = features.shape[0]
    width_local = features.shape[1]
    mp_count = lax.axis_size("mp")
    full_width = width_local * mp_count
    mp_index = lax.axis_index("mp")
    dp_index = lax.axis_index("dp")
    text_rows = texts.shape[0]
    inputs = features.astype(jnp.float32)
    mean_in = lax.psum(jnp.sum(inputs, axis=1, keepdims=True), "mp") / full_width
    centred = inputs - mean_in
    normed_b = centred.astype(jnp.bfloat16)
    partial_proj = jnp.dot(normed_b, proj_weight, preferred_element_type=jnp.float32)
    project = lax.psum(partial_proj, "mp")
    inv_norm = lax.rsqrt(jnp.sum(project * project, axis=1, keepdims=True) + epsilon)
    unit_img = project * inv_norm
    unit_img_b = unit_img.astype(jnp.bfloat16)
    image_ids = dp_index * local_rows + jnp.arange(local_rows, dtype=jnp.int32)
    piece = lax.all_gather(texts, "dp", axis=0, tiled=True)
    positions = jnp.arange(piece.shape[0], dtype=jnp.int32)
    shard_of = positions // text_rows
    piece_ids = (shard_of * mp_count + mp_index) * text_rows + positions % text_rows
    grad_unit = add_texts(unit_img_b, image_ids, piece, piece_ids)
    grad_unit = lax.psum(grad_unit, "mp")
    grad_proj = inv_norm * (
        grad_unit - unit_img * jnp.sum(unit_img * grad_unit, axis=1, keepdims=True)
    )
    grad_proj_b = grad_proj.astype(jnp.bfloat16)
    weight_part = jnp.dot(normed_b.T, grad_proj_b, preferred_element_type=jnp.float32)
    grad_weight = lax.psum(weight_part, "dp")
    grad_normed = jnp.dot(grad_proj_b, proj_weight.T, preferred_element_type=jnp.float32)
    grad_total = lax.psum(jnp.sum(grad_normed, axis=1, keepdims=True), "mp")
    grad_in = grad_normed - grad_total / full_width
    return (grad_in.astype(jnp.bfloat16), grad_weight)


def split_terms(value, count):
    terms = []
    for _ in range(count):
        term = value.astype(jnp.bfloat16).astype(jnp.float32)
        terms.append(term)
        value = value - term
    return terms


def kernel_call(body, outs, scratch=(), **names):
    return pl.pallas_call(
        body,
        out_shape=outs,
        scratch_shapes=scratch,
        compiler_params=pltpu.CompilerParams(vmem_limit_bytes=VMEM_BYTES),
        **names,
    )


def split_columns(embed):
    return embed // LANES // 3 * LANES


def texts_body(texts_ref, out_ref):
    out_ref[...] = unit_rows(texts_ref[...].astype(jnp.float32)).astype(jnp.bfloat16)


def project_body(rows, place_ref, features_ref, weight_ref, *refs):
    (*outs, extra_ref) = refs
    embed = weight_ref.shape[1]
    local_rows, width = features_ref.shape
    values = features_ref[...].astype(jnp.float32)
    row_sum = jnp.sum(values, axis=1, keepdims=True)
    column_sum = jnp.sum(weight_ref[...].astype(jnp.float32), axis=0, keepdims=True)
    extra_ref[...] = jnp.zeros_like(extra_ref)
    at = 0
    for term in split_terms(column_sum, 2):
        for i in range(embed // LANES):
            extra_ref[at : at + 1, :] = term[:, i * LANES : (i + 1) * LANES]
            at += 1
    row = lax.broadcasted_iota(jnp.int32, (local_rows, LANES), 0)
    lane = lax.broadcasted_iota(jnp.int32, (local_rows, LANES), 1)
    sum_row = jnp.sum(jnp.where(row == lane, row_sum, 0.0), axis=0, keepdims=True)
    for term in split_terms(sum_row, 3):
        extra_ref[at : at + 1, :] = term
        at += 1
    extra = extra_ref[...].astype(jnp.bfloat16)
    ordered = []
    for flip in range(len(outs)):
        start = pl.multiple_of((place_ref[0] ^ flip) * rows, rows)
        block = features_ref[pl.ds(start, rows), :].astype(jnp.float32)
        block_sum = jnp.sum(block, axis=1, keepdims=True)
        ordered.append(block - block_sum / width)
    centred = jnp.concatenate(ordered, axis=0).astype(jnp.bfloat16)
    product = jnp.dot(centred, weight_ref[...], preferred_element_type=jnp.float32)
    for flip, out_ref in enumerate(outs):
        out_ref[:, :embed] = product[flip * rows : (flip + 1) * rows].astype(jnp.bfloat16)
        out_ref[:, embed:] = extra


def unit_body(full_width, place_ref, *refs):
    (*parts, unit_b_ref, unit_ref, inv_norm_ref, mean_ref, weight_sum_ref) = refs
    rows = parts[0].shape[0]
    embed = parts[0].shape[1] - LANES
    chunks = embed // LANES
    width = full_width // len(parts)
    row = lax.broadcasted_iota(jnp.int32, (rows, LANES), 0)
    lane = lax.broadcasted_iota(jnp.int32, (rows, LANES), 1)
    mine = lane == row + place_ref[0] * rows
    project = jnp.zeros((rows, embed), jnp.float32)
    weight_sum = jnp.zeros((1, embed), jnp.float32)
    sums = []
    column_sums = []
    for part in parts:
        project = project + part[:, :embed].astype(jnp.float32)
        extra = part[:, embed:].astype(jnp.float32)
        column_sum = jnp.concatenate(
            [extra[i : i + 1] + extra[chunks + i : chunks + i + 1] for i in range(chunks)], axis=1
        )
        at = 2 * chunks
        sum_row = extra[at : at + 1] + extra[at + 1 : at + 2] + extra[at + 2 : at + 3]
        sums.append(jnp.sum(jnp.where(mine, sum_row, 0.0), axis=1, keepdims=True))
        column_sums.append(column_sum)
        weight_sum = weight_sum + column_sum
    mean = sum(sums) / full_width
    for part_sum, column_sum in zip(sums, column_sums):
        project = project + (part_sum / width - mean) * column_sum
    inv_norm = lax.rsqrt(jnp.sum(project * project, axis=1, keepdims=True) + epsilon)
    unit_img = project * inv_norm
    unit_ref[...] = unit_img
    unit_b_ref[...] = unit_img.astype(jnp.bfloat16)
    inv_norm_ref[...] = inv_norm
    mean_ref[...] = mean
    weight_sum_ref[...] = weight_sum


def slopes_body(mp_count, *refs):
    images, texts = refs[:mp_count], refs[mp_count : -mp_count]
    outs = refs[-mp_count:]
    rows = images[0].shape[0]
    unit_img_b = jnp.concatenate([ref[...] for ref in images], axis=0)
    unit_txt_b = jnp.concatenate([ref[...] for ref in texts], axis=0)
    logits = (
        logit_scale
        * lax.dot_general(
            unit_img_b,
            unit_txt_b,
            (((1,), (1,)), ((), ())),
            preferred_element_type=jnp.float32,
        )
        + logit_bias
    )
    text = lax.broadcasted_iota(jnp.int32, logits.shape, 1)
    image = lax.broadcasted_iota(jnp.int32, logits.shape, 0)
    labels = jnp.where((text == image) & (image < rows), 1.0, -1.0)
    slopes = (-labels / (1.0 + jnp.exp(labels * logits))).astype(jnp.bfloat16)
    grad_unit = logit_scale * jnp.dot(slopes, unit_txt_b, preferred_element_type=jnp.float32)
    for flip, out_ref in enumerate(outs):
        out_ref[...] = grad_unit[flip * rows : (flip + 1) * rows].astype(out_ref.dtype)


def grad_body(unit_ref, inv_norm_ref, mean_ref, *refs):
    (*parts, first_ref, second_ref) = refs
    rows, embed = unit_ref.shape
    cut = first_ref.shape[1]
    grad_unit = sum(part[...].astype(jnp.float32) for part in parts)
    unit_img = unit_ref[...]
    grad_proj = inv_norm_ref[...] * (
        grad_unit - unit_img * jnp.sum(unit_img * grad_unit, axis=1, keepdims=True)
    )
    grad_proj_b = grad_proj.astype(jnp.bfloat16)
    first_ref[...] = grad_proj_b[:, :cut]
    second_ref[:, : embed - cut] = grad_proj_b[:, cut:]
    lane = lax.broadcasted_iota(jnp.int32, (rows, LANES), 1)
    extra = jnp.zeros((rows, LANES), jnp.float32)
    for i, term in enumerate(split_terms(mean_ref[...], 3)):
        extra = jnp.where(lane == i, term, extra)
    second_ref[:, embed - cut :] = extra.astype(jnp.bfloat16)


def weight_body(
    full_width, rows, mp_count, dp_count, first_order, second_order, place_ref, weight_ref,
    weight_sum_ref, *refs
):
    (*arrays, grad_features_ref, grad_weight_ref, all_ref, normed_ref, own_ref) = refs
    features = arrays[:dp_count]
    first = arrays[dp_count : dp_count + len(first_order)]
    second = arrays[dp_count + len(first_order) :]
    embed = weight_ref.shape[1]
    cut = first[0].shape[1]
    for part, order in zip(first, first_order):
        for i, flip in enumerate(order):
            all_ref[flip * rows : (flip + 1) * rows, :cut] = part[i * rows : (i + 1) * rows, :]
    for part, order in zip(second, second_order):
        for i, flip in enumerate(order):
            here = slice(i * rows, (i + 1) * rows)
            there = slice(flip * rows, (flip + 1) * rows)
            all_ref[there, cut:] = part[here, : embed - cut]
            extra = part[here, embed - cut :].astype(jnp.float32)
            mean = extra[:, 0:1] + extra[:, 1:2] + extra[:, 2:3]
            start = pl.multiple_of((place_ref[0] ^ (flip % mp_count)) * rows, rows)
            block = features[flip // mp_count][pl.ds(start, rows), :].astype(jnp.float32)
            normed_ref[there, :] = (block - mean).astype(jnp.bfloat16)
    for flip in range(mp_count):
        start = pl.multiple_of((place_ref[0] ^ flip) * rows, rows)
        own_ref[pl.ds(start, rows), :] = all_ref[flip * rows : (flip + 1) * rows, :]
    grad_weight_ref[...] = lax.dot_general(
        normed_ref[...],
        all_ref[...],
        (((0,), (0,)), ((), ())),
        preferred_element_type=jnp.float32,
    )
    own = own_ref[...]
    grad_normed = lax.dot_general(
        own, weight_ref[...], (((1,), (1,)), ((), ())), preferred_element_type=jnp.float32
    )
    grad_total = jnp.sum(own.astype(jnp.float32) * weight_sum_ref[...], axis=1, keepdims=True)
    grad_features_ref[...] = (grad_normed - grad_total / full_width).astype(jnp.bfloat16)


def shards_gathered(features, proj_weight, texts):
    axes = ("dp", "mp")
    dp_count, mp_count = lax.axis_size("dp"), lax.axis_size("mp")
    count = dp_count * mp_count
    local_rows, width = features.shape
    embed = proj_weight.shape[1]
    rows = texts.shape[0]
    full_width = width * mp_count
    cut = split_columns(embed)
    place = lax.axis_index("mp").astype(jnp.int32).reshape(1)

    def swap(value, flip):
        return lax.ppermute(value, axes, [(i, i ^ flip) for i in range(count)])

    def struct(dims, kind=jnp.bfloat16):
        return jax.ShapeDtypeStruct(dims, kind)

    smem = pl.BlockSpec(memory_space=pltpu.SMEM)
    vmem = pl.BlockSpec(memory_space=pltpu.VMEM)
    mp_flips = range(1, mp_count)
    dp_flips = range(mp_count, count, mp_count)

    partial = kernel_call(
        functools.partial(project_body, rows),
        [struct((rows, embed + LANES))] * mp_count,
        scratch=[pltpu.VMEM((rows, LANES), jnp.float32)],
        in_specs=[smem, vmem, vmem],
        name="project",
    )(place, features, proj_weight)
    parts = [partial[0]] + [swap(partial[flip], flip) for flip in mp_flips]

    unit_txt_b = kernel_call(texts_body, struct(texts.shape), name="unit_texts")(texts)
    all_texts = [unit_txt_b] + [swap(unit_txt_b, flip) for flip in dp_flips]
    all_features = [features] + [swap(features, flip) for flip in dp_flips]

    unit_img_b, unit_img, inv_norm, mean, weight_sum = kernel_call(
        functools.partial(unit_body, full_width),
        [
            struct((rows, embed)),
            struct((rows, embed), jnp.float32),
            struct((rows, 1), jnp.float32),
            struct((rows, 1), jnp.float32),
            struct((1, embed), jnp.float32),
        ],
        in_specs=[smem] + [vmem] * mp_count,
        name="unit_images",
    )(place, *parts)
    images = [unit_img_b] + [swap(unit_img_b, flip) for flip in mp_flips]

    grad_parts = kernel_call(
        functools.partial(slopes_body, mp_count),
        [struct((rows, embed), jnp.float32)] + [struct((rows, embed))] * (mp_count - 1),
        name="slopes",
    )(*images, *all_texts)
    grad_parts = [grad_parts[0]] + [swap(grad_parts[flip], flip) for flip in mp_flips]

    first, second = kernel_call(
        grad_body,
        [struct((rows, cut)), struct((rows, embed - cut + LANES))],
        name="grad_project",
    )(unit_img, inv_norm, mean, *grad_parts)

    line = [f for f in dp_flips if f % (2 * mp_count) == 0]
    plane = [f for f in range(2, 2 * mp_count, 2)]

    def gather(value, stages):
        held, orders = [value], [[0]]
        for flips in stages:
            value = jnp.concatenate(held, axis=0) if len(held) > 1 else held[0]
            order = sum(orders, [])
            held = [value] + [swap(value, flip) for flip in flips]
            orders = [order] + [[o ^ flip for o in order] for flip in flips]
        others = [swap(value, 1) for value in held]
        return held + others, orders + [[o ^ 1 for o in order] for order in orders]

    first, first_order = gather(first, [plane, line])
    second, second_order = gather(second, [line, plane])

    return tuple(
        kernel_call(
            functools.partial(
                weight_body, full_width, rows, mp_count, dp_count, first_order, second_order
            ),
            [struct(features.shape), struct(proj_weight.shape, jnp.float32)],
            scratch=[
                pltpu.VMEM((count * rows, embed), jnp.bfloat16),
                pltpu.VMEM((count * rows, width), jnp.bfloat16),
                pltpu.VMEM((local_rows, embed), jnp.bfloat16),
            ],
            in_specs=[smem] + [vmem] * (2 + dp_count + len(first) + len(second)),
            name="weight",
        )(place, proj_weight, weight_sum, *all_features, *first, *second)
    )


def shards(features, proj_weight, texts):
    dp_count, mp_count = lax.axis_size("dp"), lax.axis_size("mp")
    count = dp_count * mp_count
    rows = texts.shape[0]
    embed = texts.shape[1]
    fits = (
        count * rows * (embed + LANES) * 2 <= GATHER_BYTES
        and count & (count - 1) == 0
        and mp_count & (mp_count - 1) == 0
        and features.shape[0] == LANES == mp_count * rows
        and embed % LANES == 0
        and 2 * (embed // LANES) + 3 <= rows
        and rows % 16 == 0
    )
    plan = shards_gathered if fits else shards_summed
    return plan(features, proj_weight, texts)


def solution(mesh):
    return jax.shard_map(
        shards,
        mesh=mesh,
        in_specs=(P("dp", "mp"), P("mp", None), P(("dp", "mp"), None)),
        out_specs=(P("dp", "mp"), P("mp", None)),
        check_vma=False,
    )
```

profile of v0, /device:TPU:0, one launch (start us, length us, event | category | flops | bytes accessed | tf_op | source)
XLA Modules:
  0.0 92.7 jit_solution(6432861111476435072)
XLA Ops:
  3.7 2.6 %collective-permute-start.1 = (bf16[32,1280]{1,0:T(8,128)(2,1)S(1)}, bf16[32,1280]{1,0:T(8,128)(2,1)S(1)}, u32[]{:S(2)}, u32[]{:S(2)}) collective-permute-start(bf16[32,1280]{1,0:T(8,128)(2,1)S(1)} %get-tuple-element.19), channel_id=1, source_target_pairs={{0,2},{1,3},{2,0},{3,1},{4,6},{5,7},{6,4},{7,5},{8,10},{9,11},{10,... | collective-permute-start | bytes 245768 | tf_op jit(solution)/shard_map/ppermute | solution.py:261
  7.4 4.8 %collective-permute-start.19 = (bf16[32,1152]{1,0:T(8,128)(2,1)S(1)}, bf16[32,1152]{1,0:T(8,128)(2,1)S(1)}, u32[]{:S(2)}, u32[]{:S(2)}) collective-permute-start(bf16[32,1152]{1,0:T(8,128)(2,1)S(1)} %unit_texts.1.refs_4_), channel_id=1, source_target_pairs={{0,28},{1,29},{2,30},{3,31},{4,24},{5,25},{6,26},{7,27},{8,20},{9,... | collective-permute-start | bytes 221192 | tf_op jit(solution)/shard_map/ppermute | solution.py:261
  13.2 2.0 %collective-permute-start.16 = (bf16[32,1152]{1,0:T(8,128)(2,1)S(1)}, bf16[32,1152]{1,0:T(8,128)(2,1)S(1)}, u32[]{:S(2)}, u32[]{:S(2)}) collective-permute-start(bf16[32,1152]{1,0:T(8,128)(2,1)S(1)} %unit_texts.1.refs_4_), channel_id=1, source_target_pairs={{0,16},{1,17},{2,18},{3,19},{4,20},{5,21},{6,22},{7,23},{8,24},{9,... | collective-permute-start | bytes 221192 | tf_op jit(solution)/shard_map/ppermute | solution.py:261
  15.2 2.4 %collective-permute-start.15 = (bf16[32,1152]{1,0:T(8,128)(2,1)S(1)}, bf16[32,1152]{1,0:T(8,128)(2,1)S(1)}, u32[]{:S(2)}, u32[]{:S(2)}) collective-permute-start(bf16[32,1152]{1,0:T(8,128)(2,1)S(1)} %unit_texts.1.refs_4_), channel_id=1, source_target_pairs={{0,12},{1,13},{2,14},{3,15},{4,8},{5,9},{6,10},{7,11},{8,4},{9,5},... | collective-permute-start | bytes 221192 | tf_op jit(solution)/shard_map/ppermute | solution.py:261
  19.8 4.4 %collective-permute-done.17.refs_9_ = bf16[32,1152]{1,0:T(8,128)(2,1)S(1)} collective-permute-done((bf16[32,1152]{1,0:T(8,128)(2,1)S(1)}, bf16[32,1152]{1,0:T(8,128)(2,1)S(1)}, u32[]{:S(2)}, u32[]{:S(2)}) %collective-permute-start.17) | collective-permute-done | bytes 73760 | tf_op jit(solution)/shard_map/ppermute | solution.py:261
  26.7 1.9 %collective-permute-done.12.refs_3_ = bf16[32,1152]{1,0:T(8,128)(2,1)S(1)} collective-permute-done((bf16[32,1152]{1,0:T(8,128)(2,1)S(1)}, bf16[32,1152]{1,0:T(8,128)(2,1)S(1)}, u32[]{:S(2)}, u32[]{:S(2)}) %collective-permute-start.12) | collective-permute-done | bytes 73760 | tf_op jit(solution)/shard_map/ppermute | solution.py:261
  28.6 1.7 %collective-permute-done.11.refs_2_ = bf16[32,1152]{1,0:T(8,128)(2,1)S(1)} collective-permute-done((bf16[32,1152]{1,0:T(8,128)(2,1)S(1)}, bf16[32,1152]{1,0:T(8,128)(2,1)S(1)}, u32[]{:S(2)}, u32[]{:S(2)}) %collective-permute-start.11) | collective-permute-done | bytes 73760 | tf_op jit(solution)/shard_map/ppermute | solution.py:261
  32.9 2.5 %collective-permute-start.8 = (bf16[128,384]{1,0:T(8,128)(2,1)S(1)}, bf16[128,384]{1,0:T(8,128)(2,1)S(1)}, u32[]{:S(2)}, u32[]{:S(2)}) collective-permute-start(bf16[128,384]{1,0:T(8,128)(2,1)S(1)} %copy-done.3), channel_id=1, source_target_pairs={{0,24},{1,25},{2,26},{3,27},{4,28},{5,29},{6,30},{7,31},{8,16},{9,... | collective-permute-start | bytes 294920 | tf_op jit(solution)/shard_map/ppermute | solution.py:261
  35.5 3.9 %collective-permute-start.6 = (bf16[128,384]{1,0:T(8,128)(2,1)S(1)}, bf16[128,384]{1,0:T(8,128)(2,1)S(1)}, u32[]{:S(2)}, u32[]{:S(2)}) collective-permute-start(bf16[128,384]{1,0:T(8,128)(2,1)S(1)} %copy-done.3), channel_id=1, source_target_pairs={{0,16},{1,17},{2,18},{3,19},{4,20},{5,21},{6,22},{7,23},{8,24},{9,... | collective-permute-start | bytes 294920 | tf_op jit(solution)/shard_map/ppermute | solution.py:261
  40.1 3.3 %collective-permute-done.23 = bf16[32,384]{1,0:T(8,128)(2,1)S(1)} collective-permute-done((bf16[32,384]{1,0:T(8,128)(2,1)S(1)}, bf16[32,384]{1,0:T(8,128)(2,1)S(1)}, u32[]{:S(2)}, u32[]{:S(2)}) %collective-permute-start.23) | collective-permute-done | bytes 24608 | tf_op jit(solution)/shard_map/ppermute | solution.py:261
  43.9 3.5 %collective-permute-done.24 = bf16[32,384]{1,0:T(8,128)(2,1)S(1)} collective-permute-done((bf16[32,384]{1,0:T(8,128)(2,1)S(1)}, bf16[32,384]{1,0:T(8,128)(2,1)S(1)}, u32[]{:S(2)}, u32[]{:S(2)}) %collective-permute-start.24) | collective-permute-done | bytes 24608 | tf_op jit(solution)/shard_map/ppermute | solution.py:261
  48.1 4.0 %collective-permute-done.25 = bf16[32,384]{1,0:T(8,128)(2,1)S(1)} collective-permute-done((bf16[32,384]{1,0:T(8,128)(2,1)S(1)}, bf16[32,384]{1,0:T(8,128)(2,1)S(1)}, u32[]{:S(2)}, u32[]{:S(2)}) %collective-permute-start.25) | collective-permute-done | bytes 24608 | tf_op jit(solution)/shard_map/ppermute | solution.py:261
  52.1 1.8 %collective-permute-start.33 = (bf16[32,896]{1,0:T(8,128)(2,1)S(1)}, bf16[32,896]{1,0:T(8,128)(2,1)S(1)}, u32[]{:S(2)}, u32[]{:S(2)}) collective-permute-start(bf16[32,896]{1,0:T(8,128)(2,1)S(1)} %get-tuple-element.31), channel_id=1, source_target_pairs={{0,8},{1,9},{2,10},{3,11},{4,12},{5,13},{6,14},{7,15},{8,0},{9,1},... | collective-permute-start | bytes 172040 | tf_op jit(solution)/shard_map/ppermute | solution.py:261
  53.9 2.4 %collective-permute-done.33 = bf16[32,896]{1,0:T(8,128)(2,1)S(1)} collective-permute-done((bf16[32,896]{1,0:T(8,128)(2,1)S(1)}, bf16[32,896]{1,0:T(8,128)(2,1)S(1)}, u32[]{:S(2)}, u32[]{:S(2)}) %collective-permute-start.33) | collective-permute-done | bytes 57376 | tf_op jit(solution)/shard_map/ppermute | solution.py:261
  56.3 1.6 %collective-permute-start.34 = (bf16[32,896]{1,0:T(8,128)(2,1)S(1)}, bf16[32,896]{1,0:T(8,128)(2,1)S(1)}, u32[]{:S(2)}, u32[]{:S(2)}) collective-permute-start(bf16[32,896]{1,0:T(8,128)(2,1)S(1)} %get-tuple-element.31), channel_id=1, source_target_pairs={{0,16},{1,17},{2,18},{3,19},{4,20},{5,21},{6,22},{7,23},{8,24},{9,... | collective-permute-start | bytes 172040 | tf_op jit(solution)/shard_map/ppermute | solution.py:261
  57.9 4.0 %collective-permute-done.34 = bf16[32,896]{1,0:T(8,128)(2,1)S(1)} collective-permute-done((bf16[32,896]{1,0:T(8,128)(2,1)S(1)}, bf16[32,896]{1,0:T(8,128)(2,1)S(1)}, u32[]{:S(2)}, u32[]{:S(2)}) %collective-permute-start.34) | collective-permute-done | bytes 57376 | tf_op jit(solution)/shard_map/ppermute | solution.py:261
  61.9 3.1 %collective-permute-start.35 = (bf16[32,896]{1,0:T(8,128)(2,1)S(1)}, bf16[32,896]{1,0:T(8,128)(2,1)S(1)}, u32[]{:S(2)}, u32[]{:S(2)}) collective-permute-start(bf16[32,896]{1,0:T(8,128)(2,1)S(1)} %get-tuple-element.31), channel_id=1, source_target_pairs={{0,24},{1,25},{2,26},{3,27},{4,28},{5,29},{6,30},{7,31},{8,16},{9,... | collective-permute-start | bytes 172040 | tf_op jit(solution)/shard_map/ppermute | solution.py:261
  65.8 2.0 %collective-permute-start.9 = (bf16[128,384]{1,0:T(8,128)(2,1)S(1)}, bf16[128,384]{1,0:T(8,128)(2,1)S(1)}, u32[]{:S(2)}, u32[]{:S(2)}) collective-permute-start(bf16[128,384]{1,0:T(8,128)(2,1)S(1)} %copy-done.3), channel_id=1, source_target_pairs={{0,28},{1,29},{2,30},{3,31},{4,24},{5,25},{6,26},{7,27},{8,20},{9,... | collective-permute-start | bytes 294920 | tf_op jit(solution)/shard_map/ppermute | solution.py:261
  67.9 1.9 %collective-permute-start.38 = (bf16[128,896]{1,0:T(8,128)(2,1)S(1)}, bf16[128,896]{1,0:T(8,128)(2,1)S(1)}, u32[]{:S(2)}, u32[]{:S(2)}) collective-permute-start(bf16[128,896]{1,0:T(8,128)(2,1)S(1)} %constant_dynamic-update-slice_fusion.4.refs_16_), channel_id=1, source_target_pairs={{0,6},{1,7},{2,4},{3,5},{4,2},{5,3},{6,0},{7,1},{8,14},{9,15},{10,... | collective-permute-start | bytes 688136 | tf_op jit(solution)/shard_map/ppermute | solution.py:261
  73.2 2.5 %collective-permute-start.28 = (bf16[128,384]{1,0:T(8,128)(2,1)S(1)}, bf16[128,384]{1,0:T(8,128)(2,1)S(1)}, u32[]{:S(2)}, u32[]{:S(2)}) collective-permute-start(bf16[128,384]{1,0:T(8,128)(2,1)S(1)} %constant_dynamic-update-slice_fusion.refs_8_), channel_id=1, source_target_pairs={{0,24},{1,25},{2,26},{3,27},{4,28},{5,29},{6,30},{7,31},{8,16},{9,... | collective-permute-start | bytes 294920 | tf_op jit(solution)/shard_map/ppermute | solution.py:261
  75.7 3.9 %collective-permute-done.28.refs_11_ = bf16[128,384]{1,0:T(8,128)(2,1)S(1)} collective-permute-done((bf16[128,384]{1,0:T(8,128)(2,1)S(1)}, bf16[128,384]{1,0:T(8,128)(2,1)S(1)}, u32[]{:S(2)}, u32[]{:S(2)}) %collective-permute-start.28) | collective-permute-done | bytes 98336 | tf_op jit(solution)/shard_map/ppermute | solution.py:261
  79.6 3.3 %collective-permute-start.26 = (bf16[128,384]{1,0:T(8,128)(2,1)S(1)}, bf16[128,384]{1,0:T(8,128)(2,1)S(1)}, u32[]{:S(2)}, u32[]{:S(2)}) collective-permute-start(bf16[128,384]{1,0:T(8,128)(2,1)S(1)} %constant_dynamic-update-slice_fusion.refs_8_), channel_id=1, source_target_pairs={{0,8},{1,9},{2,10},{3,11},{4,12},{5,13},{6,14},{7,15},{8,0},{9,1},... | collective-permute-start | bytes 294920 | tf_op jit(solution)/shard_map/ppermute | solution.py:261
  83.4 2.0 %collective-permute-done.26.refs_9_ = bf16[128,384]{1,0:T(8,128)(2,1)S(1)} collective-permute-done((bf16[128,384]{1,0:T(8,128)(2,1)S(1)}, bf16[128,384]{1,0:T(8,128)(2,1)S(1)}, u32[]{:S(2)}, u32[]{:S(2)}) %collective-permute-start.26) | collective-permute-done | bytes 98336 | tf_op jit(solution)/shard_map/ppermute | solution.py:261
  89.4 3.3 %weight.1 = (bf16[128,384]{1,0:T(8,128)(2,1)}, f32[384,1152]{1,0:T(8,128)}) custom-call(s32[1]{0:T(128)} %bitcast.place_ref, bf16[384,1152]{1,0:T(8,128)(2,1)S(1)} %copy-done.1, f32[1,1152]{1,0:T(1,128)S(1)} %get-tuple-element.21.weight_sum_ref, bf16[128,384]{1,0:T(8,128)(2,1)S(1)} %copy-done.3, bf16[128,384]{1,0:T(8,128)(2,1)S(1)} %collective-permute-done.3.refs_1_, ...), custom_call_target="tpu_custom_call" | custom-call | tf_op jit(solution)/shard_map/weight/pallas_call | solution.py:328
  (86 shorter events, 23.3 us)
Async XLA Ops:
  3.2 9.2 %collective-permute-start = (bf16[32,1280]{1,0:T(8,128)(2,1)S(1)}, bf16[32,1280]{1,0:T(8,128)(2,1)S(1)}, u32[]{:S(2)}, u32[]{:S(2)}) collective-permute-start(bf16[32,1280]{1,0:T(8,128)(2,1)S(1)} %get-tuple-element.18), channel_id=1, source_target_pairs={{0,1},{1,0},{2,3},{3,2},{4,5},{5,4},{6,7},{7,6},{8,9},{9,8},{10,11... | collective-permute-start | bytes 245768 | tf_op jit(solution)/shard_map/ppermute | solution.py:261
  3.7 9.5 %collective-permute-start.1 = (bf16[32,1280]{1,0:T(8,128)(2,1)S(1)}, bf16[32,1280]{1,0:T(8,128)(2,1)S(1)}, u32[]{:S(2)}, u32[]{:S(2)}) collective-permute-start(bf16[32,1280]{1,0:T(8,128)(2,1)S(1)} %get-tuple-element.19), channel_id=1, source_target_pairs={{0,2},{1,3},{2,0},{3,1},{4,6},{5,7},{6,4},{7,5},{8,10},{9,11},{10,... | collective-permute-start | bytes 245768 | tf_op jit(solution)/shard_map/ppermute | solution.py:261
  6.3 8.9 %collective-permute-start.2 = (bf16[32,1280]{1,0:T(8,128)(2,1)S(1)}, bf16[32,1280]{1,0:T(8,128)(2,1)S(1)}, u32[]{:S(2)}, u32[]{:S(2)}) collective-permute-start(bf16[32,1280]{1,0:T(8,128)(2,1)S(1)} %get-tuple-element.20), channel_id=1, source_target_pairs={{0,3},{1,2},{2,1},{3,0},{4,7},{5,6},{6,5},{7,4},{8,11},{9,10},{10,... | collective-permute-start | bytes 245768 | tf_op jit(solution)/shard_map/ppermute | solution.py:261
  7.4 10.4 %collective-permute-start.19 = (bf16[32,1152]{1,0:T(8,128)(2,1)S(1)}, bf16[32,1152]{1,0:T(8,128)(2,1)S(1)}, u32[]{:S(2)}, u32[]{:S(2)}) collective-permute-start(bf16[32,1152]{1,0:T(8,128)(2,1)S(1)} %unit_texts.1.refs_4_), channel_id=1, source_target_pairs={{0,28},{1,29},{2,30},{3,31},{4,24},{5,25},{6,26},{7,27},{8,20},{9,... | collective-permute-start | bytes 221192 | tf_op jit(solution)/shard_map/ppermute | solution.py:261
  12.2 7.0 %collective-permute-start.18 = (bf16[32,1152]{1,0:T(8,128)(2,1)S(1)}, bf16[32,1152]{1,0:T(8,128)(2,1)S(1)}, u32[]{:S(2)}, u32[]{:S(2)}) collective-permute-start(bf16[32,1152]{1,0:T(8,128)(2,1)S(1)} %unit_texts.1.refs_4_), channel_id=1, source_target_pairs={{0,24},{1,25},{2,26},{3,27},{4,28},{5,29},{6,30},{7,31},{8,16},{9,... | collective-permute-start | bytes 221192 | tf_op jit(solution)/shard_map/ppermute | solution.py:261
  12.4 11.7 %collective-permute-start.17 = (bf16[32,1152]{1,0:T(8,128)(2,1)S(1)}, bf16[32,1152]{1,0:T(8,128)(2,1)S(1)}, u32[]{:S(2)}, u32[]{:S(2)}) collective-permute-start(bf16[32,1152]{1,0:T(8,128)(2,1)S(1)} %unit_texts.1.refs_4_), channel_id=1, source_target_pairs={{0,20},{1,21},{2,22},{3,23},{4,16},{5,17},{6,18},{7,19},{8,28},{9,... | collective-permute-start | bytes 221192 | tf_op jit(solution)/shard_map/ppermute | solution.py:261
  13.2 12.0 %collective-permute-start.16 = (bf16[32,1152]{1,0:T(8,128)(2,1)S(1)}, bf16[32,1152]{1,0:T(8,128)(2,1)S(1)}, u32[]{:S(2)}, u32[]{:S(2)}) collective-permute-start(bf16[32,1152]{1,0:T(8,128)(2,1)S(1)} %unit_texts.1.refs_4_), channel_id=1, source_target_pairs={{0,16},{1,17},{2,18},{3,19},{4,20},{5,21},{6,22},{7,23},{8,24},{9,... | collective-permute-start | bytes 221192 | tf_op jit(solution)/shard_map/ppermute | solution.py:261
  15.2 11.5 %collective-permute-start.15 = (bf16[32,1152]{1,0:T(8,128)(2,1)S(1)}, bf16[32,1152]{1,0:T(8,128)(2,1)S(1)}, u32[]{:S(2)}, u32[]{:S(2)}) collective-permute-start(bf16[32,1152]{1,0:T(8,128)(2,1)S(1)} %unit_texts.1.refs_4_), channel_id=1, source_target_pairs={{0,12},{1,13},{2,14},{3,15},{4,8},{5,9},{6,10},{7,11},{8,4},{9,5},... | collective-permute-start | bytes 221192 | tf_op jit(solution)/shard_map/ppermute | solution.py:261
  17.8 8.9 %collective-permute-start.14 = (bf16[32,1152]{1,0:T(8,128)(2,1)S(1)}, bf16[32,1152]{1,0:T(8,128)(2,1)S(1)}, u32[]{:S(2)}, u32[]{:S(2)}) collective-permute-start(bf16[32,1152]{1,0:T(8,128)(2,1)S(1)} %unit_texts.1.refs_4_), channel_id=1, source_target_pairs={{0,8},{1,9},{2,10},{3,11},{4,12},{5,13},{6,14},{7,15},{8,0},{9,1},... | collective-permute-start | bytes 221192 | tf_op jit(solution)/shard_map/ppermute | solution.py:261
  19.2 7.5 %collective-permute-start.13 = (bf16[32,1152]{1,0:T(8,128)(2,1)S(1)}, bf16[32,1152]{1,0:T(8,128)(2,1)S(1)}, u32[]{:S(2)}, u32[]{:S(2)}) collective-permute-start(bf16[32,1152]{1,0:T(8,128)(2,1)S(1)} %unit_texts.1.refs_4_), channel_id=1, source_target_pairs={{0,4},{1,5},{2,6},{3,7},{4,0},{5,1},{6,2},{7,3},{8,12},{9,13},{10,... | collective-permute-start | bytes 221192 | tf_op jit(solution)/shard_map/ppermute | solution.py:261
  31.1 8.3 %collective-permute-start.21 = (bf16[32,1152]{1,0:T(8,128)(2,1)S(1)}, bf16[32,1152]{1,0:T(8,128)(2,1)S(1)}, u32[]{:S(2)}, u32[]{:S(2)}) collective-permute-start(bf16[32,1152]{1,0:T(8,128)(2,1)S(1)} %get-tuple-element.28), channel_id=1, source_target_pairs={{0,2},{1,3},{2,0},{3,1},{4,6},{5,7},{6,4},{7,5},{8,10},{9,11},{10,... | collective-permute-start | bytes 221192 | tf_op jit(solution)/shard_map/ppermute | solution.py:261
  31.9 7.4 %collective-permute-start.22 = (bf16[32,1152]{1,0:T(8,128)(2,1)S(1)}, bf16[32,1152]{1,0:T(8,128)(2,1)S(1)}, u32[]{:S(2)}, u32[]{:S(2)}) collective-permute-start(bf16[32,1152]{1,0:T(8,128)(2,1)S(1)} %get-tuple-element.29), channel_id=1, source_target_pairs={{0,3},{1,2},{2,1},{3,0},{4,7},{5,6},{6,5},{7,4},{8,11},{9,10},{10,... | collective-permute-start | bytes 221192 | tf_op jit(solution)/shard_map/ppermute | solution.py:261
  32.9 32.1 %collective-permute-start.8 = (bf16[128,384]{1,0:T(8,128)(2,1)S(1)}, bf16[128,384]{1,0:T(8,128)(2,1)S(1)}, u32[]{:S(2)}, u32[]{:S(2)}) collective-permute-start(bf16[128,384]{1,0:T(8,128)(2,1)S(1)} %copy-done.3), channel_id=1, source_target_pairs={{0,24},{1,25},{2,26},{3,27},{4,28},{5,29},{6,30},{7,31},{8,16},{9,... | collective-permute-start | bytes 294920 | tf_op jit(solution)/shard_map/ppermute | solution.py:261
  35.5 29.6 %collective-permute-start.7 = (bf16[128,384]{1,0:T(8,128)(2,1)S(1)}, bf16[128,384]{1,0:T(8,128)(2,1)S(1)}, u32[]{:S(2)}, u32[]{:S(2)}) collective-permute-start(bf16[128,384]{1,0:T(8,128)(2,1)S(1)} %copy-done.3), channel_id=1, source_target_pairs={{0,20},{1,21},{2,22},{3,23},{4,16},{5,17},{6,18},{7,19},{8,28},{9,... | collective-permute-start | bytes 294920 | tf_op jit(solution)/shard_map/ppermute | solution.py:261
  35.5 30.3 %collective-permute-start.6 = (bf16[128,384]{1,0:T(8,128)(2,1)S(1)}, bf16[128,384]{1,0:T(8,128)(2,1)S(1)}, u32[]{:S(2)}, u32[]{:S(2)}) collective-permute-start(bf16[128,384]{1,0:T(8,128)(2,1)S(1)} %copy-done.3), channel_id=1, source_target_pairs={{0,16},{1,17},{2,18},{3,19},{4,20},{5,21},{6,22},{7,23},{8,24},{9,... | collective-permute-start | bytes 294920 | tf_op jit(solution)/shard_map/ppermute | solution.py:261
  39.3 28.6 %collective-permute-start.5 = (bf16[128,384]{1,0:T(8,128)(2,1)S(1)}, bf16[128,384]{1,0:T(8,128)(2,1)S(1)}, u32[]{:S(2)}, u32[]{:S(2)}) collective-permute-start(bf16[128,384]{1,0:T(8,128)(2,1)S(1)} %copy-done.3), channel_id=1, source_target_pairs={{0,12},{1,13},{2,14},{3,15},{4,8},{5,9},{6,10},{7,11},{8,4},{9,5},... | collective-permute-start | bytes 294920 | tf_op jit(solution)/shard_map/ppermute | solution.py:261
  61.9 6.0 %collective-permute-start.35 = (bf16[32,896]{1,0:T(8,128)(2,1)S(1)}, bf16[32,896]{1,0:T(8,128)(2,1)S(1)}, u32[]{:S(2)}, u32[]{:S(2)}) collective-permute-start(bf16[32,896]{1,0:T(8,128)(2,1)S(1)} %get-tuple-element.31), channel_id=1, source_target_pairs={{0,24},{1,25},{2,26},{3,27},{4,28},{5,29},{6,30},{7,31},{8,16},{9,... | collective-permute-start | bytes 172040 | tf_op jit(solution)/shard_map/ppermute | solution.py:261
  65.8 7.4 %collective-permute-start.9 = (bf16[128,384]{1,0:T(8,128)(2,1)S(1)}, bf16[128,384]{1,0:T(8,128)(2,1)S(1)}, u32[]{:S(2)}, u32[]{:S(2)}) collective-permute-start(bf16[128,384]{1,0:T(8,128)(2,1)S(1)} %copy-done.3), channel_id=1, source_target_pairs={{0,28},{1,29},{2,30},{3,31},{4,24},{5,25},{6,26},{7,27},{8,20},{9,... | collective-permute-start | bytes 294920 | tf_op jit(solution)/shard_map/ppermute | solution.py:261
  67.9 7.8 %collective-permute-start.29 = (bf16[128,384]{1,0:T(8,128)(2,1)S(1)}, bf16[128,384]{1,0:T(8,128)(2,1)S(1)}, u32[]{:S(2)}, u32[]{:S(2)}) collective-permute-start(bf16[128,384]{1,0:T(8,128)(2,1)S(1)} %constant_dynamic-update-slice_fusion.refs_8_), channel_id=1, source_target_pairs={{0,1},{1,0},{2,3},{3,2},{4,5},{5,4},{6,7},{7,6},{8,9},{9,8},{10,11... | collective-permute-start | bytes 294920 | tf_op jit(solution)/shard_map/ppermute | solution.py:261
  67.9 17.5 %collective-permute-start.38 = (bf16[128,896]{1,0:T(8,128)(2,1)S(1)}, bf16[128,896]{1,0:T(8,128)(2,1)S(1)}, u32[]{:S(2)}, u32[]{:S(2)}) collective-permute-start(bf16[128,896]{1,0:T(8,128)(2,1)S(1)} %constant_dynamic-update-slice_fusion.4.refs_16_), channel_id=1, source_target_pairs={{0,6},{1,7},{2,4},{3,5},{4,2},{5,3},{6,0},{7,1},{8,14},{9,15},{10,... | collective-permute-start | bytes 688136 | tf_op jit(solution)/shard_map/ppermute | solution.py:261
  69.8 16.1 %collective-permute-start.37 = (bf16[128,896]{1,0:T(8,128)(2,1)S(1)}, bf16[128,896]{1,0:T(8,128)(2,1)S(1)}, u32[]{:S(2)}, u32[]{:S(2)}) collective-permute-start(bf16[128,896]{1,0:T(8,128)(2,1)S(1)} %constant_dynamic-update-slice_fusion.4.refs_16_), channel_id=1, source_target_pairs={{0,4},{1,5},{2,6},{3,7},{4,0},{5,1},{6,2},{7,3},{8,12},{9,13},{10,... | collective-permute-start | bytes 688136 | tf_op jit(solution)/shard_map/ppermute | solution.py:261
  70.9 15.2 %collective-permute-start.36 = (bf16[128,896]{1,0:T(8,128)(2,1)S(1)}, bf16[128,896]{1,0:T(8,128)(2,1)S(1)}, u32[]{:S(2)}, u32[]{:S(2)}) collective-permute-start(bf16[128,896]{1,0:T(8,128)(2,1)S(1)} %constant_dynamic-update-slice_fusion.4.refs_16_), channel_id=1, source_target_pairs={{0,2},{1,3},{2,0},{3,1},{4,6},{5,7},{6,4},{7,5},{8,10},{9,11},{10,... | collective-permute-start | bytes 688136 | tf_op jit(solution)/shard_map/ppermute | solution.py:261
  73.2 6.4 %collective-permute-start.28 = (bf16[128,384]{1,0:T(8,128)(2,1)S(1)}, bf16[128,384]{1,0:T(8,128)(2,1)S(1)}, u32[]{:S(2)}, u32[]{:S(2)}) collective-permute-start(bf16[128,384]{1,0:T(8,128)(2,1)S(1)} %constant_dynamic-update-slice_fusion.refs_8_), channel_id=1, source_target_pairs={{0,24},{1,25},{2,26},{3,27},{4,28},{5,29},{6,30},{7,31},{8,16},{9,... | collective-permute-start | bytes 294920 | tf_op jit(solution)/shard_map/ppermute | solution.py:261
  75.7 7.8 %collective-permute-start.27 = (bf16[128,384]{1,0:T(8,128)(2,1)S(1)}, bf16[128,384]{1,0:T(8,128)(2,1)S(1)}, u32[]{:S(2)}, u32[]{:S(2)}) collective-permute-start(bf16[128,384]{1,0:T(8,128)(2,1)S(1)} %constant_dynamic-update-slice_fusion.refs_8_), channel_id=1, source_target_pairs={{0,16},{1,17},{2,18},{3,19},{4,20},{5,21},{6,22},{7,23},{8,24},{9,... | collective-permute-start | bytes 294920 | tf_op jit(solution)/shard_map/ppermute | solution.py:261
  (24 other events, 197.0 us)
where the time goes:
time: 93 us; the launch traced here: 92.7 us
  starting transfers between devices  46.5 us (50%)
  waiting for transfers between devices  37.5 us (40%)
  Pallas kernels  4.99 us (5%)
  local copies, waits for them, and re-layouts  3.02 us (3%)
    ppermute x43, starting transfers between devices, swap(): return lax.ppermute(value, axes, [(i, i ^ flip) for i in range(count)])  46.5 us
    ppermute x43, waiting for transfers between devices, swap(): return lax.ppermute(value, axes, [(i, i ^ flip) for i in range(count)])  37.5 us
    pallas_call x1, Pallas kernels, shards_gathered(): kernel_call(functools.partial(weight_body, full_width, rows, mp_count, dp...  3.33 us
    unnamed x16, local copies, waits for them, and re-layouts  2.99 us
  transfers between devices with their start and end apart: 43, of which 17 were waited for; matrix products, arithmetic and copies ran while one was open for 0% of the time, Pallas kernels for 1%

commit v1 on v0

v1 whole, which is shorter than its diff:
```python
import functools

import jax
import jax.numpy as jnp
from jax import lax
from jax.experimental import pallas as pl
from jax.experimental.pallas import tpu as pltpu
from jax.sharding import PartitionSpec as P

logit_scale = 100.0
logit_bias = -10.0
epsilon = 1e-06
LANES = 128
GATHER_BYTES = 8 << 20
VMEM_BYTES = 40 << 20


def unit_rows(values):
    return values * lax.rsqrt(jnp.sum(values * values, axis=1, keepdims=True) + epsilon)


def add_texts(unit_img_b, image_ids, piece, piece_ids):
    unit_txt_b = unit_rows(piece.astype(jnp.float32)).astype(jnp.bfloat16)
    logits = (
        logit_scale * jnp.dot(unit_img_b, unit_txt_b.T, preferred_element_type=jnp.float32)
        + logit_bias
    )
    labels = jnp.where(image_ids[:, None] == piece_ids[None, :], 1.0, -1.0).astype(jnp.float32)
    slopes = (-labels * jax.nn.sigmoid(-labels * logits)).astype(jnp.bfloat16)
    return logit_scale * jnp.dot(slopes, unit_txt_b, preferred_element_type=jnp.float32)


def shards_summed(features, proj_weight, texts):
    local_rows = features.shape[0]
    width_local = features.shape[1]
    mp_count = lax.axis_size("mp")
    full_width = width_local * mp_count
    mp_index = lax.axis_index("mp")
    dp_index = lax.axis_index("dp")
    text_rows = texts.shape[0]
    inputs = features.astype(jnp.float32)
    mean_in = lax.psum(jnp.sum(inputs, axis=1, keepdims=True), "mp") / full_width
    centred = inputs - mean_in
    normed_b = centred.astype(jnp.bfloat16)
    partial_proj = jnp.dot(normed_b, proj_weight, preferred_element_type=jnp.float32)
    project = lax.psum(partial_proj, "mp")
    inv_norm = lax.rsqrt(jnp.sum(project * project, axis=1, keepdims=True) + epsilon)
    unit_img = project * inv_norm
    unit_img_b = unit_img.astype(jnp.bfloat16)
    image_ids = dp_index * local_rows + jnp.arange(local_rows, dtype=jnp.int32)
    piece = lax.all_gather(texts, "dp", axis=0, tiled=True)
    positions = jnp.arange(piece.shape[0], dtype=jnp.int32)
    shard_of = positions // text_rows
    piece_ids = (shard_of * mp_count + mp_index) * text_rows + positions % text_rows
    grad_unit = add_texts(unit_img_b, image_ids, piece, piece_ids)
    grad_unit = lax.psum(grad_unit, "mp")
    grad_proj = inv_norm * (
        grad_unit - unit_img * jnp.sum(unit_img * grad_unit, axis=1, keepdims=True)
    )
    grad_proj_b = grad_proj.astype(jnp.bfloat16)
    weight_part = jnp.dot(normed_b.T, grad_proj_b, preferred_element_type=jnp.float32)
    grad_weight = lax.psum(weight_part, "dp")
    grad_normed = jnp.dot(grad_proj_b, proj_weight.T, preferred_element_type=jnp.float32)
    grad_total = lax.psum(jnp.sum(grad_normed, axis=1, keepdims=True), "mp")
    grad_in = grad_normed - grad_total / full_width
    return (grad_in.astype(jnp.bfloat16), grad_weight)


def split_terms(value, count):
    terms = []
    for _ in range(count):
        term = value.astype(jnp.bfloat16).astype(jnp.float32)
        terms.append(term)
        value = value - term
    return terms


def kernel_call(body, outs, scratch=(), **names):
    return pl.pallas_call(
        body,
        out_shape=outs,
        scratch_shapes=scratch,
        compiler_params=pltpu.CompilerParams(vmem_limit_bytes=VMEM_BYTES),
        **names,
    )


def texts_body(texts_ref, out_ref):
    out_ref[...] = unit_rows(texts_ref[...].astype(jnp.float32)).astype(jnp.bfloat16)


def project_body(rows, features_ref, weight_ref, out_ref, extra_ref):
    embed = weight_ref.shape[1]
    local_rows, width = features_ref.shape
    values = features_ref[...].astype(jnp.float32)
    row_sum = jnp.sum(values, axis=1, keepdims=True)
    column_sum = jnp.sum(weight_ref[...].astype(jnp.float32), axis=0, keepdims=True)
    extra_ref[...] = jnp.zeros_like(extra_ref)
    at = 0
    for term in split_terms(column_sum, 2):
        for i in range(embed // LANES):
            extra_ref[at : at + 1, :] = term[:, i * LANES : (i + 1) * LANES]
            at += 1
    row = lax.broadcasted_iota(jnp.int32, (local_rows, LANES), 0)
    lane = lax.broadcasted_iota(jnp.int32, (local_rows, LANES), 1)
    sum_row = jnp.sum(jnp.where(row == lane, row_sum, 0.0), axis=0, keepdims=True)
    for term in split_terms(sum_row, 3):
        extra_ref[at : at + 1, :] = term
        at += 1
    centred = (values - row_sum / width).astype(jnp.bfloat16)
    product = jnp.dot(centred, weight_ref[...], preferred_element_type=jnp.float32)
    out_ref[:, :embed] = product.astype(jnp.bfloat16)
    extra = extra_ref[...].astype(jnp.bfloat16)
    for i in range(local_rows // rows):
        out_ref[i * rows : (i + 1) * rows, embed:] = extra


def unit_body(full_width, mp_count, place_ref, parts_ref, *refs):
    (unit_b_ref, unit_ref, inv_norm_ref, mean_ref, weight_sum_ref) = refs
    rows = parts_ref.shape[0] // mp_count
    embed = parts_ref.shape[1] - LANES
    chunks = embed // LANES
    width = full_width // mp_count
    row = lax.broadcasted_iota(jnp.int32, (rows, LANES), 0)
    lane = lax.broadcasted_iota(jnp.int32, (rows, LANES), 1)
    mine = lane == row + (place_ref[0] & (mp_count - 1)) * rows
    project = jnp.zeros((rows, embed), jnp.float32)
    weight_sum = jnp.zeros((1, embed), jnp.float32)
    sums = []
    column_sums = []
    for k in range(mp_count):
        part = parts_ref[k * rows : (k + 1) * rows, :].astype(jnp.float32)
        project = project + part[:, :embed]
        extra = part[:, embed:]
        column_sum = jnp.concatenate(
            [extra[i : i + 1] + extra[chunks + i : chunks + i + 1] for i in range(chunks)], axis=1
        )
        at = 2 * chunks
        sum_row = extra[at : at + 1] + extra[at + 1 : at + 2] + extra[at + 2 : at + 3]
        sums.append(jnp.sum(jnp.where(mine, sum_row, 0.0), axis=1, keepdims=True))
        column_sums.append(column_sum)
        weight_sum = weight_sum + column_sum
    mean = sum(sums) / full_width
    for part_sum, column_sum in zip(sums, column_sums):
        project = project + (part_sum / width - mean) * column_sum
    inv_norm = lax.rsqrt(jnp.sum(project * project, axis=1, keepdims=True) + epsilon)
    unit_img = project * inv_norm
    unit_ref[...] = unit_img
    unit_img_b = unit_img.astype(jnp.bfloat16)
    for k in range(mp_count):
        unit_b_ref[k * rows : (k + 1) * rows, :] = unit_img_b
    inv_norm_ref[...] = inv_norm
    mean_ref[...] = mean
    weight_sum_ref[...] = weight_sum


def slopes_body(mp_count, place_ref, images_ref, *refs):
    (*texts, out_ref) = refs
    rows = images_ref.shape[0] // mp_count
    unit_txt_b = jnp.concatenate([ref[...] for ref in texts], axis=0)
    logits = (
        logit_scale
        * lax.dot_general(
            images_ref[...],
            unit_txt_b,
            (((1,), (1,)), ((), ())),
            preferred_element_type=jnp.float32,
        )
        + logit_bias
    )
    text = lax.broadcasted_iota(jnp.int32, logits.shape, 1)
    image = lax.broadcasted_iota(jnp.int32, logits.shape, 0)
    own = (place_ref[0] & (mp_count - 1)) * rows
    labels = jnp.where((text + own == image) & (text < rows), 1.0, -1.0)
    slopes = (-labels / (1.0 + jnp.exp(labels * logits))).astype(jnp.bfloat16)
    grad_unit = logit_scale * jnp.dot(slopes, unit_txt_b, preferred_element_type=jnp.float32)
    out_ref[...] = grad_unit.astype(out_ref.dtype)


def grad_body(copies, mp_count, unit_ref, inv_norm_ref, mean_ref, parts_ref, out_ref):
    rows, embed = unit_ref.shape
    grad_unit = jnp.zeros((rows, embed), jnp.float32)
    for k in range(mp_count):
        grad_unit = grad_unit + parts_ref[k * rows : (k + 1) * rows, :].astype(jnp.float32)
    unit_img = unit_ref[...]
    grad_proj = inv_norm_ref[...] * (
        grad_unit - unit_img * jnp.sum(unit_img * grad_unit, axis=1, keepdims=True)
    )
    grad_proj_b = grad_proj.astype(jnp.bfloat16)
    lane = lax.broadcasted_iota(jnp.int32, (rows, LANES), 1)
    extra = jnp.zeros((rows, LANES), jnp.float32)
    for i, term in enumerate(split_terms(mean_ref[...], 3)):
        extra = jnp.where(lane == i, term, extra)
    extra = extra.astype(jnp.bfloat16)
    for k in range(copies):
        out_ref[k * rows : (k + 1) * rows, :embed] = grad_proj_b
        out_ref[k * rows : (k + 1) * rows, embed:] = extra


def weight_body(full_width, rows, mp_count, line_count, place_ref, weight_ref, weight_sum_ref,
                features_a_ref, features_b_ref, own_ref, other_ref, *refs):
    (grad_features_ref, grad_weight_ref, all_ref, normed_ref, group_ref) = refs
    embed = weight_ref.shape[1]
    here = place_ref[0]
    plane = 2 * mp_count
    for flip in range(plane * line_count):
        device = here ^ flip
        at = ((device & (plane - 1)) >> 1) * line_count + device // plane
        part_ref = other_ref if flip & 1 else own_ref
        part = part_ref[pl.ds(pl.multiple_of(at * rows, rows), rows), :]
        there = slice(flip * rows, (flip + 1) * rows)
        all_ref[there, :] = part[:, :embed]
        extra = part[:, embed:].astype(jnp.float32)
        mean = extra[:, 0:1] + extra[:, 1:2] + extra[:, 2:3]
        features_ref = features_b_ref if flip & mp_count else features_a_ref
        start = (flip // plane) * mp_count * rows + (device & (mp_count - 1)) * rows
        block = features_ref[pl.ds(pl.multiple_of(start, rows), rows), :].astype(jnp.float32)
        normed_ref[there, :] = (block - mean).astype(jnp.bfloat16)
        if flip < mp_count:
            start = pl.multiple_of((device & (mp_count - 1)) * rows, rows)
            group_ref[pl.ds(start, rows), :] = part[:, :embed]
    grad_weight_ref[...] = lax.dot_general(
        normed_ref[...],
        all_ref[...],
        (((0,), (0,)), ((), ())),
        preferred_element_type=jnp.float32,
    )
    group = group_ref[...]
    grad_normed = lax.dot_general(
        group, weight_ref[...], (((1,), (1,)), ((), ())), preferred_element_type=jnp.float32
    )
    grad_total = jnp.sum(group.astype(jnp.float32) * weight_sum_ref[...], axis=1, keepdims=True)
    grad_features_ref[...] = (grad_normed - grad_total / full_width).astype(jnp.bfloat16)


def shards_gathered(features, proj_weight, texts):
    axes = ("dp", "mp")
    dp_count, mp_count = lax.axis_size("dp"), lax.axis_size("mp")
    count = dp_count * mp_count
    plane_count = 2 * mp_count
    line_count = count // plane_count
    local_rows, width = features.shape
    embed = proj_weight.shape[1]
    rows = texts.shape[0]
    full_width = width * mp_count
    place = (lax.axis_index("dp") * mp_count + lax.axis_index("mp")).astype(jnp.int32).reshape(1)

    def swap(value, flip):
        return lax.ppermute(value, axes, [(i, i ^ flip) for i in range(count)])

    def exchange(value, flips=None):
        if flips is None:
            return lax.all_to_all(value, "mp", 0, 0, tiled=True)
        mask = functools.reduce(lambda x, y: x | y, flips)
        groups = [sorted(i ^ f for f in flips) for i in range(count) if i & mask == 0]
        return lax.all_to_all(value, axes, 0, 0, tiled=True, axis_index_groups=groups)

    def struct(dims, kind=jnp.bfloat16):
        return jax.ShapeDtypeStruct(dims, kind)

    smem = pl.BlockSpec(memory_space=pltpu.SMEM)
    vmem = pl.BlockSpec(memory_space=pltpu.VMEM)
    line = list(range(0, count, plane_count))
    plane = list(range(0, plane_count, 2))

    unit_txt_b = kernel_call(texts_body, struct(texts.shape), name="unit_texts")(texts)
    line_texts = [unit_txt_b] + [swap(unit_txt_b, flip) for flip in line[1:]]
    line_texts = jnp.concatenate(line_texts, axis=0)
    all_texts = [line_texts, swap(line_texts, mp_count)]

    line_features = [features] + [swap(features, flip) for flip in line[1:]]
    line_features = jnp.concatenate(line_features, axis=0)

    partial = kernel_call(
        functools.partial(project_body, rows),
        struct((local_rows, embed + LANES)),
        scratch=[pltpu.VMEM((rows, LANES), jnp.float32)],
        name="project",
    )(features, proj_weight)
    parts = exchange(partial)

    unit_img_b, unit_img, inv_norm, mean, weight_sum = kernel_call(
        functools.partial(unit_body, full_width, mp_count),
        [
            struct((local_rows, embed)),
            struct((rows, embed), jnp.float32),
            struct((rows, 1), jnp.float32),
            struct((rows, 1), jnp.float32),
            struct((1, embed), jnp.float32),
        ],
        in_specs=[smem, vmem],
        name="unit_images",
    )(place, parts)
    images = exchange(unit_img_b)
    images, line_features = lax.optimization_barrier((images, line_features))

    other_features = swap(line_features, mp_count)
    grad_parts = kernel_call(
        functools.partial(slopes_body, mp_count),
        struct((local_rows, embed)),
        in_specs=[smem] + [vmem] * 3,
        name="slopes",
    )(place, images, *all_texts)
    grad_parts = exchange(grad_parts)
    grad_parts, other_features = lax.optimization_barrier((grad_parts, other_features))

    grad_rows = kernel_call(
        functools.partial(grad_body, line_count, mp_count),
        struct((line_count * rows, embed + LANES)),
        name="grad_project",
    )(unit_img, inv_norm, mean, grad_parts)

    grad_rows = exchange(grad_rows, line)
    grad_rows = exchange(jnp.concatenate([grad_rows] * len(plane), axis=0), plane)
    grad_others = swap(grad_rows, 1)

    return tuple(
        kernel_call(
            functools.partial(weight_body, full_width, rows, mp_count, line_count),
            [struct(features.shape), struct(proj_weight.shape, jnp.float32)],
            scratch=[
                pltpu.VMEM((count * rows, embed), jnp.bfloat16),
                pltpu.VMEM((count * rows, width), jnp.bfloat16),
                pltpu.VMEM((local_rows, embed), jnp.bfloat16),
            ],
            in_specs=[smem] + [vmem] * 6,
            name="weight",
        )(place, proj_weight, weight_sum, line_features, other_features, grad_rows, grad_others)
    )


def shards(features, proj_weight, texts):
    dp_count, mp_count = lax.axis_size("dp"), lax.axis_size("mp")
    count = dp_count * mp_count
    rows = texts.shape[0]
    embed = texts.shape[1]
    fits = (
        count * rows * (embed + LANES) * 2 <= GATHER_BYTES
        and count & (count - 1) == 0
        and mp_count & (mp_count - 1) == 0
        and features.shape[0] == LANES == mp_count * rows
        and embed % LANES == 0
        and 2 * (embed // LANES) + 3 <= rows
        and rows % 16 == 0
    )
    plan = shards_gathered if fits else shards_summed
    return plan(features, proj_weight, texts)


def solution(mesh):
    return jax.shard_map(
        shards,
        mesh=mesh,
        in_specs=(P("dp", "mp"), P("mp", None), P(("dp", "mp"), None)),
        out_specs=(P("dp", "mp"), P("mp", None)),
        check_vma=False,
    )
```

time: 93 us -> 82.7 us (0.89)
  blocking collectives: 0 us -> 41.5 us
  waiting for transfers between devices: 37.5 us -> 9.79 us
  starting transfers between devices: 46.5 us -> 21.7 us
  Pallas kernels: 4.99 us -> 6.32 us
  local copies, waits for them, and re-layouts: 3.02 us -> 2.07 us
    all_to_all x0 -> x3, blocking collectives: none -> 41.5 us  [the longest x2 32.1 us: exchange(): lax.all_to_all(value, axes, 0, 0, tiled=True, axis_index_groups=groups)]
    ppermute x43 -> x9, starting transfers between devices: 46.5 us -> 14 us  [swap(): return lax.ppermute(value, axes, [(i, i ^ flip) for i in range(count)])]
    ppermute x43 -> x9, waiting for transfers between devices: 37.5 us -> 9.79 us  [swap(): return lax.ppermute(value, axes, [(i, i ^ flip) for i in range(count)])]
    all_to_all x0 -> x2, starting transfers between devices: none -> 7.69 us  [exchange(): return lax.all_to_all(value, 'mp', 0, 0, tiled=True)]
    pallas_call x5, Pallas kernels: 4.88 us -> 6.21 us  [the longest x1 3.18 us: shards_gathered(): kernel_call(functools.partial(weight_body, full_width, rows, mp_count, li...]
    unnamed x16 -> x10, local copies, waits for them, and re-layouts: 2.99 us -> 2.07 us
  transfers between devices with their start and end apart: 43 -> 11, of which waited for: 17 -> 3; matrix products, arithmetic and copies ran while one was open for 0% -> 0% of each run, Pallas kernels for 1% -> 2%
where the time goes in v1:
time: 82.7 us; the launch traced here: 82.3 us
  blocking collectives  41.5 us (50%)
  starting transfers between devices  21.7 us (26%)
  waiting for transfers between devices  9.79 us (12%)
  Pallas kernels  6.32 us (8%)
  local copies, waits for them, and re-layouts  2.07 us (3%)
    all_to_all x2, blocking collectives, exchange(): lax.all_to_all(value, axes, 0, 0, tiled=True, axis_index_groups=groups)  32.1 us
    ppermute x9, starting transfers between devices, swap(): return lax.ppermute(value, axes, [(i, i ^ flip) for i in range(count)])  14 us
    ppermute x9, waiting for transfers between devices, swap(): return lax.ppermute(value, axes, [(i, i ^ flip) for i in range(count)])  9.79 us
    all_to_all x1, blocking collectives, exchange(): return lax.all_to_all(value, 'mp', 0, 0, tiled=True)  9.42 us
    all_to_all x2, starting transfers between devices, exchange(): return lax.all_to_all(value, 'mp', 0, 0, tiled=True)  7.69 us
    pallas_call x1, Pallas kernels, shards_gathered(): kernel_call(functools.partial(weight_body, full_width, rows, mp_count, li...  3.18 us
    unnamed x10, local copies, waits for them, and re-layouts  2.07 us
  transfers between devices with their start and end apart: 11, of which 3 were waited for; matrix products, arithmetic and copies ran while one was open for 0% of the time, Pallas kernels for 2%

profile of v1, /device:TPU:0, one launch (start us, length us, event | category | flops | bytes accessed | tf_op | source)
XLA Modules:
  0.0 82.3 jit_solution(3486428277662220112)
XLA Ops:
  0.6 1.2 %copy-done = bf16[384,1152]{1,0:T(8,128)(2,1)S(1)} copy-done((bf16[384,1152]{1,0:T(8,128)(2,1)S(1)}, bf16[384,1152]{1,0:T(8,128)(2,1)}, u32[]{:S(2)}) %copy-start) | copy-done | bytes 884760
  1.8 0.9 %copy-done.2 = bf16[128,384]{1,0:T(8,128)(2,1)S(1)} copy-done((bf16[128,384]{1,0:T(8,128)(2,1)S(1)}, bf16[128,384]{1,0:T(8,128)(2,1)}, u32[]{:S(2)}) %copy-start.2) | copy-done | bytes 98328
  2.7 1.2 %project.1 = bf16[128,1280]{1,0:T(8,128)(2,1)} custom-call(bf16[128,384]{1,0:T(8,128)(2,1)S(1)} %copy-done.2, bf16[384,1152]{1,0:T(8,128)(2,1)S(1)} %copy-done), custom_call_target="tpu_custom_call" | custom-call | tf_op jit(solution)/shard_map/project/pallas_call | solution.py:274
  3.9 4.2 %all-to-all-start = ((bf16[4,32,1280]{2,1,0:T(8,128)(2,1)}), bf16[4,32,1280]{2,1,0:T(8,128)(2,1)S(1)}, u32[]{:S(2)}, u32[]{:S(2)}) async-start(bf16[4,32,1280]{2,1,0:T(8,128)(2,1)} %bitcast.1), calls=%async_computation | async-start | bytes 655360 | tf_op jit(solution)/shard_map/all_to_all | solution.py:253
  8.2 0.1 unit_texts.1
  8.3 4.3 %collective-permute-start.5 = (bf16[32,1152]{1,0:T(8,128)(2,1)S(1)}, bf16[32,1152]{1,0:T(8,128)(2,1)S(1)}, u32[]{:S(2)}, u32[]{:S(2)}) collective-permute-start(bf16[32,1152]{1,0:T(8,128)(2,1)S(1)} %unit_texts.1), channel_id=1, source_target_pairs={{0,24},{1,25},{2,26},{3,27},{4,28},{5,29},{6,30},{7,31},{8,16},{9,... | collective-permute-start | bytes 221192 | tf_op jit(solution)/shard_map/ppermute | solution.py:249
  12.6 0.6 collective-permute-start.3
  13.3 2.3 %collective-permute-start.1 = (bf16[128,384]{1,0:T(8,128)(2,1)S(1)}, bf16[128,384]{1,0:T(8,128)(2,1)S(1)}, u32[]{:S(2)}, u32[]{:S(2)}) collective-permute-start(bf16[128,384]{1,0:T(8,128)(2,1)S(1)} %copy-done.3), channel_id=1, source_target_pairs={{0,16},{1,17},{2,18},{3,19},{4,20},{5,21},{6,22},{7,23},{8,24},{9,... | collective-permute-start | bytes 294920 | tf_op jit(solution)/shard_map/ppermute | solution.py:249
  15.6 2.0 %collective-permute-start = (bf16[128,384]{1,0:T(8,128)(2,1)S(1)}, bf16[128,384]{1,0:T(8,128)(2,1)S(1)}, u32[]{:S(2)}, u32[]{:S(2)}) collective-permute-start(bf16[128,384]{1,0:T(8,128)(2,1)S(1)} %copy-done.3), channel_id=1, source_target_pairs={{0,8},{1,9},{2,10},{3,11},{4,12},{5,13},{6,14},{7,15},{8,0},{9,1},... | collective-permute-start | bytes 294920 | tf_op jit(solution)/shard_map/ppermute | solution.py:249
  17.6 1.0 %unit_images.1 = (bf16[128,1152]{1,0:T(8,128)(2,1)}, f32[32,1152]{1,0:T(8,128)S(1)}, f32[32,1]{1,0:T(8,128)S(1)}, f32[32,1]{1,0:T(8,128)S(1)}, f32[1,1152]{1,0:T(1,128)S(1)}) custom-call(s32[1]{0:T(128)} %bitcast.place_ref, bf16[128,1280]{1,0:T(8,128)(2,1)S(1)} %bitcast.14), custom_call_target="tpu_custom_call" | custom-call | tf_op jit(solution)/shard_map/unit_images/pallas_call | solution.py:282
  18.6 3.5 %all-to-all-start.1 = ((bf16[4,32,1152]{2,1,0:T(8,128)(2,1)}), bf16[4,32,1152]{2,1,0:T(8,128)(2,1)S(1)}, u32[]{:S(2)}, u32[]{:S(2)}) async-start(bf16[4,32,1152]{2,1,0:T(8,128)(2,1)} %bitcast.3), calls=%async_computation.1 | async-start | bytes 589824 | tf_op jit(solution)/shard_map/all_to_all | solution.py:253
  22.0 1.6 %collective-permute-start.2 = (bf16[128,384]{1,0:T(8,128)(2,1)S(1)}, bf16[128,384]{1,0:T(8,128)(2,1)S(1)}, u32[]{:S(2)}, u32[]{:S(2)}) collective-permute-start(bf16[128,384]{1,0:T(8,128)(2,1)S(1)} %copy-done.3), channel_id=1, source_target_pairs={{0,24},{1,25},{2,26},{3,27},{4,28},{5,29},{6,30},{7,31},{8,16},{9,... | collective-permute-start | bytes 294920 | tf_op jit(solution)/shard_map/ppermute | solution.py:249
  23.7 1.6 %collective-permute-start.6 = (bf16[128,1152]{1,0:T(8,128)(2,1)S(1)}, bf16[128,1152]{1,0:T(8,128)(2,1)S(1)}, u32[]{:S(2)}, u32[]{:S(2)}) collective-permute-start(bf16[128,1152]{1,0:T(8,128)(2,1)S(1)} %pad_maximum_fusion.2.refs_0_), channel_id=1, source_target_pairs={{0,4},{1,5},{2,6},{3,7},{4,0},{5,1},{6,2},{7,3},{8,12},{9,13},{10,... | collective-permute-start | bytes 884744 | tf_op jit(solution)/shard_map/ppermute | solution.py:249
  25.3 3.8 %collective-permute-done.2 = bf16[128,384]{1,0:T(8,128)(2,1)S(1)} collective-permute-done((bf16[128,384]{1,0:T(8,128)(2,1)S(1)}, bf16[128,384]{1,0:T(8,128)(2,1)S(1)}, u32[]{:S(2)}, u32[]{:S(2)}) %collective-permute-start.2) | collective-permute-done | bytes 98336 | tf_op jit(solution)/shard_map/ppermute | solution.py:249
  29.1 1.6 %collective-permute-start.7 = (bf16[512,384]{1,0:T(8,128)(2,1)S(1)}, bf16[512,384]{1,0:T(8,128)(2,1)S(1)}, u32[]{:S(2)}, u32[]{:S(2)}) collective-permute-start(bf16[512,384]{1,0:T(8,128)(2,1)S(1)} %pad_maximum_fusion.1.features_a_ref), channel_id=1, source_target_pairs={{0,4},{1,5},{2,6},{3,7},{4,0},{5,1},{6,2},{7,3},{8,12},{9,13},{10,... | collective-permute-start | bytes 1179656 | tf_op jit(solution)/shard_map/ppermute | solution.py:249
  30.6 3.0 %collective-permute-done.6.refs_1_ = bf16[128,1152]{1,0:T(8,128)(2,1)S(1)} collective-permute-done((bf16[128,1152]{1,0:T(8,128)(2,1)S(1)}, bf16[128,1152]{1,0:T(8,128)(2,1)S(1)}, u32[]{:S(2)}, u32[]{:S(2)}) %collective-permute-start.6) | collective-permute-done | bytes 294944 | tf_op jit(solution)/shard_map/ppermute | solution.py:249
  33.6 0.7 slopes.1
  34.3 9.4 %all_to_all.58 = bf16[4,32,1152]{2,1,0:T(8,128)(2,1)S(1)} all-to-all(bf16[4,32,1152]{2,1,0:T(8,128)(2,1)S(1)} %bitcast.17), channel_id=1, replica_groups=mesh['dp'=8,'mp'=4] {'mp'}, dimensions={0} | all-to-all | bytes 589824 | tf_op jit(solution)/shard_map/all_to_all | solution.py:253
  43.7 0.1 grad_project.1
  43.9 13.8 %all_to_all.59 = bf16[4,32,1280]{2,1,0:T(8,128)(2,1)S(1)} all-to-all(bf16[4,32,1280]{2,1,0:T(8,128)(2,1)S(1)} %bitcast.13), channel_id=1, replica_groups={{0,8,16,24},{1,9,17,25},{2,10,18,26},{3,11,19,27},{4,12,20,28},{5,13,21..., dimensions={0} | all-to-all | bytes 655360 | tf_op jit(solution)/shard_map/all_to_all | solution.py:256
  57.6 0.1 pad_maximum_fusion
  57.7 18.3 %all_to_all.60 = bf16[4,128,1280]{2,1,0:T(8,128)(2,1)S(1)} all-to-all(bf16[4,128,1280]{2,1,0:T(8,128)(2,1)S(1)} %bitcast.18), channel_id=1, replica_groups={{0,2,4,6},{1,3,5,7},{8,10,12,14},{9,11,13,15},{16,18,20,22},{17,19,21,2..., dimensions={0} | all-to-all | bytes 2621440 | tf_op jit(solution)/shard_map/all_to_all | solution.py:256
  76.0 3.0 %collective-permute-done.8.other_ref = bf16[512,1280]{1,0:T(8,128)(2,1)S(1)} collective-permute-done((bf16[512,1280]{1,0:T(8,128)(2,1)S(1)}, bf16[512,1280]{1,0:T(8,128)(2,1)S(1)}, u32[]{:S(2)}, u32[]{:S(2)}) %collective-permute-start.8) | collective-permute-done | bytes 1310752 | tf_op jit(solution)/shard_map/ppermute | solution.py:249
  79.1 3.2 %weight.1 = (bf16[128,384]{1,0:T(8,128)(2,1)}, f32[384,1152]{1,0:T(8,128)}) custom-call(s32[1]{0:T(128)} %bitcast.place_ref, bf16[384,1152]{1,0:T(8,128)(2,1)S(1)} %copy-done.1, f32[1,1152]{1,0:T(1,128)S(1)} %get-tuple-element.11.weight_sum_ref, bf16[512,384]{1,0:T(8,128)(2,1)S(1)} %pad_maximum_fusion.1.features_a_ref, ...), custom_call_target="tpu_custom_call" | custom-call | tf_op jit(solution)/shard_map/weight/pallas_call | solution.py:318
  (20 shorter events, 0.1 us)
Async XLA Ops:
  0.6 1.2 %copy-start = (bf16[384,1152]{1,0:T(8,128)(2,1)S(1)}, bf16[384,1152]{1,0:T(8,128)(2,1)}, u32[]{:S(2)}) copy-start(bf16[384,1152]{1,0:T(8,128)(2,1)} %weight_ref.3) | copy-start | bytes 2654212
  1.8 0.9 %copy-start.2 = (bf16[128,384]{1,0:T(8,128)(2,1)S(1)}, bf16[128,384]{1,0:T(8,128)(2,1)}, u32[]{:S(2)}) copy-start(bf16[128,384]{1,0:T(8,128)(2,1)} %features_ref.1) | copy-start | bytes 294916
  2.7 5.5 %copy-start.4 = (bf16[32,1152]{1,0:T(8,128)(2,1)S(1)}, bf16[32,1152]{1,0:T(8,128)(2,1)}, u32[]{:S(2)}) copy-start(bf16[32,1152]{1,0:T(8,128)(2,1)} %texts_ref.1) | copy-start | bytes 221188
  2.7 10.6 %copy-start.3 = (bf16[128,384]{1,0:T(8,128)(2,1)S(1)}, bf16[128,384]{1,0:T(8,128)(2,1)}, u32[]{:S(2)}) copy-start(bf16[128,384]{1,0:T(8,128)(2,1)} %features_ref.1) | copy-start | bytes 294916
  3.9 13.7 %all-to-all-start = ((bf16[4,32,1280]{2,1,0:T(8,128)(2,1)}), bf16[4,32,1280]{2,1,0:T(8,128)(2,1)S(1)}, u32[]{:S(2)}, u32[]{:S(2)}) async-start(bf16[4,32,1280]{2,1,0:T(8,128)(2,1)} %bitcast.1), calls=%async_computation | async-start | bytes 655360 | tf_op jit(solution)/shard_map/all_to_all | solution.py:253
  8.3 13.7 %collective-permute-start.5 = (bf16[32,1152]{1,0:T(8,128)(2,1)S(1)}, bf16[32,1152]{1,0:T(8,128)(2,1)S(1)}, u32[]{:S(2)}, u32[]{:S(2)}) collective-permute-start(bf16[32,1152]{1,0:T(8,128)(2,1)S(1)} %unit_texts.1), channel_id=1, source_target_pairs={{0,24},{1,25},{2,26},{3,27},{4,28},{5,29},{6,30},{7,31},{8,16},{9,... | collective-permute-start | bytes 221192 | tf_op jit(solution)/shard_map/ppermute | solution.py:249
  12.6 11.0 %collective-permute-start.4 = (bf16[32,1152]{1,0:T(8,128)(2,1)S(1)}, bf16[32,1152]{1,0:T(8,128)(2,1)S(1)}, u32[]{:S(2)}, u32[]{:S(2)}) collective-permute-start(bf16[32,1152]{1,0:T(8,128)(2,1)S(1)} %unit_texts.1), channel_id=1, source_target_pairs={{0,16},{1,17},{2,18},{3,19},{4,20},{5,21},{6,22},{7,23},{8,24},{9,... | collective-permute-start | bytes 221192 | tf_op jit(solution)/shard_map/ppermute | solution.py:249
  12.6 11.0 %collective-permute-start.3 = (bf16[32,1152]{1,0:T(8,128)(2,1)S(1)}, bf16[32,1152]{1,0:T(8,128)(2,1)S(1)}, u32[]{:S(2)}, u32[]{:S(2)}) collective-permute-start(bf16[32,1152]{1,0:T(8,128)(2,1)S(1)} %unit_texts.1), channel_id=1, source_target_pairs={{0,8},{1,9},{2,10},{3,11},{4,12},{5,13},{6,14},{7,15},{8,0},{9,1},... | collective-permute-start | bytes 221192 | tf_op jit(solution)/shard_map/ppermute | solution.py:249
  13.3 12.0 %collective-permute-start.1 = (bf16[128,384]{1,0:T(8,128)(2,1)S(1)}, bf16[128,384]{1,0:T(8,128)(2,1)S(1)}, u32[]{:S(2)}, u32[]{:S(2)}) collective-permute-start(bf16[128,384]{1,0:T(8,128)(2,1)S(1)} %copy-done.3), channel_id=1, source_target_pairs={{0,16},{1,17},{2,18},{3,19},{4,20},{5,21},{6,22},{7,23},{8,24},{9,... | collective-permute-start | bytes 294920 | tf_op jit(solution)/shard_map/ppermute | solution.py:249
  15.6 9.7 %collective-permute-start = (bf16[128,384]{1,0:T(8,128)(2,1)S(1)}, bf16[128,384]{1,0:T(8,128)(2,1)S(1)}, u32[]{:S(2)}, u32[]{:S(2)}) collective-permute-start(bf16[128,384]{1,0:T(8,128)(2,1)S(1)} %copy-done.3), channel_id=1, source_target_pairs={{0,8},{1,9},{2,10},{3,11},{4,12},{5,13},{6,14},{7,15},{8,0},{9,1},... | collective-permute-start | bytes 294920 | tf_op jit(solution)/shard_map/ppermute | solution.py:249
  18.6 10.5 %all-to-all-start.1 = ((bf16[4,32,1152]{2,1,0:T(8,128)(2,1)}), bf16[4,32,1152]{2,1,0:T(8,128)(2,1)S(1)}, u32[]{:S(2)}, u32[]{:S(2)}) async-start(bf16[4,32,1152]{2,1,0:T(8,128)(2,1)} %bitcast.3), calls=%async_computation.1 | async-start | bytes 589824 | tf_op jit(solution)/shard_map/all_to_all | solution.py:253
  22.0 7.0 %collective-permute-start.2 = (bf16[128,384]{1,0:T(8,128)(2,1)S(1)}, bf16[128,384]{1,0:T(8,128)(2,1)S(1)}, u32[]{:S(2)}, u32[]{:S(2)}) collective-permute-start(bf16[128,384]{1,0:T(8,128)(2,1)S(1)} %copy-done.3), channel_id=1, source_target_pairs={{0,24},{1,25},{2,26},{3,27},{4,28},{5,29},{6,30},{7,31},{8,16},{9,... | collective-permute-start | bytes 294920 | tf_op jit(solution)/shard_map/ppermute | solution.py:249
  23.7 9.9 %collective-permute-start.6 = (bf16[128,1152]{1,0:T(8,128)(2,1)S(1)}, bf16[128,1152]{1,0:T(8,128)(2,1)S(1)}, u32[]{:S(2)}, u32[]{:S(2)}) collective-permute-start(bf16[128,1152]{1,0:T(8,128)(2,1)S(1)} %pad_maximum_fusion.2.refs_0_), channel_id=1, source_target_pairs={{0,4},{1,5},{2,6},{3,7},{4,0},{5,1},{6,2},{7,3},{8,12},{9,13},{10,... | collective-permute-start | bytes 884744 | tf_op jit(solution)/shard_map/ppermute | solution.py:249
  29.1 14.6 %collective-permute-start.7 = (bf16[512,384]{1,0:T(8,128)(2,1)S(1)}, bf16[512,384]{1,0:T(8,128)(2,1)S(1)}, u32[]{:S(2)}, u32[]{:S(2)}) collective-permute-start(bf16[512,384]{1,0:T(8,128)(2,1)S(1)} %pad_maximum_fusion.1.features_a_ref), channel_id=1, source_target_pairs={{0,4},{1,5},{2,6},{3,7},{4,0},{5,1},{6,2},{7,3},{8,12},{9,13},{10,... | collective-permute-start | bytes 1179656 | tf_op jit(solution)/shard_map/ppermute | solution.py:249
  57.6 21.4 %copy-start.1 = (bf16[384,1152]{1,0:T(8,128)(2,1)S(1)}, bf16[384,1152]{1,0:T(8,128)(2,1)}, u32[]{:S(2)}) copy-start(bf16[384,1152]{1,0:T(8,128)(2,1)} %weight_ref.3) | copy-start | bytes 2654212
  76.0 3.0 %collective-permute-start.8 = (bf16[512,1280]{1,0:T(8,128)(2,1)S(1)}, bf16[512,1280]{1,0:T(8,128)(2,1)S(1)}, u32[]{:S(2)}, u32[]{:S(2)}) collective-permute-start(bf16[512,1280]{1,0:T(8,128)(2,1)S(1)} %bitcast.11), channel_id=1, source_target_pairs={{0,1},{1,0},{2,3},{3,2},{4,5},{5,4},{6,7},{7,6},{8,9},{9,8},{10,11... | collective-permute-start | bytes 3932168 | tf_op jit(solution)/shard_map/ppermute | solution.py:249
